TPU v7x, 32 devices: a whole 2x2x4 slice. The times are simulated.
32 devices in a mesh: sweep: 8 (over y, x, core), span: 4 (over z).
Axes of the slice: x: 2, y: 2, z: 4, core: 2. Of those that a mesh axis runs over, the one named last changes fastest.
Arguments:
- inverses: bfloat16 [8, 4, 6, 135, 135], P('sweep', 'span')
- couplings: bfloat16 [6, 8, 4, 6, 135, 135], P(None, 'sweep', 'span')
- rhs: bfloat16 [8, 4, 6, 135, 128], P('sweep', 'span'), may hold values from -6 to 6
- previous: bfloat16 [8, 4, 6, 135, 128], P('sweep', 'span'), may hold values from -6 to 6
- slot_layer: int32 [8, 4, 6], P('sweep', 'span'), may hold values from 0 to 5, each once within a row
Outputs:
- solution: float32 [8, 4, 6, 135, 128], P('sweep', 'span')
Inputs may be any that keep to these rules, and one draw needn't show every extreme that they name: `slot_layer`: in each line each wall-normal layer is stored in exactly one slot.
All inputs are finite; a program needn't handle non-finite values.
Results may differ from a plain program's by a relative error of at most 0.0029.
Values may be sent and summed in bfloat16 or wider, within the bound.
A program may use at most 128 MiB of HBM per device.

v0:
```python
import functools

import jax
import jax.numpy as jnp
from jax import lax
from jax.experimental import pallas as pl
from jax.experimental.pallas import tpu as pltpu
from jax.sharding import PartitionSpec as P

MESH = pl.DeviceIdType.MESH


def split(value):
    high = value.astype(jnp.bfloat16)
    low = (value - high.astype(jnp.float32)).astype(jnp.bfloat16)
    return high, low


def mul(a, b):
    return jnp.dot(a, b, preferred_element_type=jnp.float32)


def kernel(
    planes, lines,
    layer, inv_hbm, coup_hbm, rhs_hbm, prev_hbm,
    out,
    inv, coup, rhs, prev, lower, upper, down,
    high, low, mate_high, mate_low, both_high, both_low,
    part, offset, mate, inflow, fresh, rows,
    load_sem, store_sem, halo_send, halo_recv, map_send, map_recv,
    mate_send, mate_recv, pass_send, relay_send, relay_recv,
):
    slots, size, width = prev.shape
    me = lax.axis_index("sweep")
    line = lax.axis_index("span")
    odd = lax.rem(me, 2) == 1
    even = jnp.logical_not(odd)
    first = me < 2
    later = jnp.logical_not(first)
    has_up = me > 0
    has_after = me < planes - 1
    takes = jnp.logical_and(odd, later)
    gives = jnp.logical_and(odd, me < planes - 2)
    left = {"span": lax.rem(line + lines - 1, lines)}
    right = {"span": lax.rem(line + 1, lines)}
    up = {"sweep": jnp.maximum(me - 1, 0)}
    after = {"sweep": jnp.minimum(me + 1, planes - 1)}
    behind = {"sweep": jnp.maximum(me - 2, 0)}
    ahead = {"sweep": jnp.minimum(me + 2, planes - 1)}

    pairs = [(prev_hbm, prev), (inv_hbm, inv), (rhs_hbm, rhs)]
    loads = [
        pltpu.make_async_copy(a, b, load_sem.at[k]) for k, (a, b) in enumerate(pairs)
    ]
    faces = [
        pltpu.make_async_copy(coup_hbm.at[f], coup.at[f], load_sem.at[len(pairs) + f])
        for f in range(6)
    ]
    for copy in (loads[1], faces[0], loads[0], faces[4], faces[5], loads[2]):
        copy.start()
    for copy in faces[1:4]:
        copy.start()

    barrier = pltpu.get_barrier_semaphore()

    def greet(device):
        pl.semaphore_signal(barrier, inc=1, device_id=device, device_id_type=MESH)

    greet(left)
    greet(right)
    expected = jnp.int32(2)
    for there, device in ((has_up, up), (has_after, after), (takes, behind), (gives, ahead)):
        pl.when(there)(functools.partial(greet, device))
        expected = expected + there.astype(jnp.int32)
    pl.semaphore_wait(barrier, expected)

    def send(src, dst, send_sem, recv_sem, device):
        return pltpu.make_async_remote_copy(
            src_ref=src,
            dst_ref=dst,
            send_sem=send_sem,
            recv_sem=recv_sem,
            device_id=device,
            device_id_type=MESH,
        )

    def halo(kind, s):
        target, ref = ((right, lower), (left, upper), (up, down))[kind]
        return send(prev_hbm.at[s], ref.at[s], halo_send.at[kind, s], halo_recv.at[kind, s], target)

    def give_map(k):
        src, dst = ((high, mate_high), (low, mate_low))[k]
        return send(src, dst, map_send.at[k], map_recv.at[k], after)

    def give_offset(s):
        return send(offset.at[s], mate.at[s], mate_send.at[s], mate_recv.at[s], after)

    def pass_on(s):
        return send(inflow.at[s], inflow.at[s], pass_send.at[s], relay_recv.at[s], up)

    def relay(s):
        return send(fresh.at[s], inflow.at[s], relay_send.at[s], relay_recv.at[s], ahead)

    for s in range(slots):
        halo(0, s).start()
        halo(1, s).start()

    @pl.when(has_up)
    def _():
        for s in range(slots):
            halo(2, s).start()

    @pl.when(jnp.logical_not(has_after))
    def _():
        down[...] = jnp.zeros_like(down)

    loads[1].wait()
    faces[0].wait()
    for s in range(slots):
        high[s], low[s] = split(-mul(inv[s], coup[0, s]))

    @pl.when(jnp.logical_and(even, later))
    def _():
        give_map(0).start()
        give_map(1).start()

    loads[0].wait()
    faces[4].wait()
    faces[5].wait()
    loads[2].wait()

    for s in range(slots):
        total = rhs[s].astype(jnp.float32)
        for face, step in ((4, -1), (5, 1)):
            wanted = layer[s] + step
            found = jnp.int32(0)
            known = jnp.int32(0)
            for t in range(slots):
                hit = (layer[t] == wanted).astype(jnp.int32)
                found = found + t * hit
                known = known + hit
            vector = prev[found].astype(jnp.float32) * known.astype(jnp.float32)
            total = total - mul(coup[face, s], vector.astype(jnp.bfloat16))
        part[s] = total

    for copy in faces[1:4]:
        copy.wait()

    @pl.when(takes)
    def _():
        give_map(0).wait_recv()
        give_map(1).wait_recv()
        for s in range(slots):
            one, two = mate_high[s], mate_low[s]
            product = mul(high[s], one) + (mul(high[s], two) + mul(low[s], one))
            both_high[s], both_low[s] = split(product)

    def apply_map(matrix_high, matrix_low, vector):
        one, two = split(vector)
        wide = mul(matrix_high, jnp.concatenate([one, two], axis=1))
        return wide[:, :width] + (wide[:, width:] + mul(matrix_low, one))

    def store(s):
        return pltpu.make_async_copy(rows.at[s], out.at[s], store_sem.at[s])

    def put(s, value):
        rows[s, :, 0, :] = value
        store(s).start()

    for k in range(slots + 1):
        if k < slots:
            s = k
            halo(0, s).wait_recv()
            halo(1, s).wait_recv()
            pl.when(has_after)(halo(2, s).wait_recv)
            coupled = mul(coup[1, s], down[s])
            coupled = coupled + mul(coup[2, s], lower[s])
            coupled = coupled + mul(coup[3, s], upper[s])
            forcing = (part[s] - coupled).astype(jnp.bfloat16)
            offset[s] = mul(inv[s], forcing)
            pl.when(even)(give_offset(s).start)

            @pl.when(odd)
            def _(s=s):
                give_offset(s).wait_recv()
                fresh[s] = offset[s] + apply_map(high[s], low[s], mate[s])

            @pl.when(jnp.logical_and(odd, first))
            def _(s=s):
                pl.when(gives)(relay(s).start)
                put(s, fresh[s])

        if k > 0:
            s = k - 1

            @pl.when(takes)
            def _(s=s):
                relay(s).wait_recv()
                pass_on(s).start()
                fresh[s] = fresh[s] + apply_map(both_high[s], both_low[s], inflow[s])
                pl.when(gives)(relay(s).start)
                put(s, fresh[s])

    @pl.when(even)
    def _():
        @pl.when(first)
        def _():
            for s in range(slots):
                put(s, offset[s])

        @pl.when(later)
        def _():
            for s in range(slots):
                relay(s).wait_recv()
                put(s, offset[s] + apply_map(high[s], low[s], inflow[s]))
            give_map(0).wait_send()
            give_map(1).wait_send()

        for s in range(slots):
            give_offset(s).wait_send()

    for s in range(slots):
        store(s).wait()
        halo(0, s).wait_send()
        halo(1, s).wait_send()

    @pl.when(has_up)
    def _():
        for s in range(slots):
            halo(2, s).wait_send()

    @pl.when(takes)
    def _():
        for s in range(slots):
            pass_on(s).wait_send()

    @pl.when(gives)
    def _():
        for s in range(slots):
            relay(s).wait_send()


def move(src, dst, held, load_sem, store_sem):
    slots = src.shape[0]
    loads = [
        pltpu.make_async_copy(src.at[s], held.at[s], load_sem.at[s]) for s in range(slots)
    ]
    stores = [
        pltpu.make_async_copy(held.at[s], dst.at[s], store_sem.at[s]) for s in range(slots)
    ]
    for load in loads:
        load.start()
    for load, store in zip(loads, stores):
        load.wait()
        store.start()
    for store in stores:
        store.wait()


def solution(mesh):
    planes, lines = mesh.shape["sweep"], mesh.shape["span"]

    def local(inverses, couplings, rhs, previous, slot_layer):
        slots, size, width = previous.shape[2:]
        inverses = inverses.reshape(slots, size, size)
        couplings = couplings.reshape(6, slots, size, size)
        flat = (slots, size, width)
        hbm = pl.BlockSpec(memory_space=pl.ANY)
        smem = pl.BlockSpec(memory_space=pltpu.SMEM)
        thin = pltpu.VMEM(flat, jnp.bfloat16)
        wide = pltpu.VMEM(flat, jnp.float32)
        square = pltpu.VMEM((slots, size, size), jnp.bfloat16)
        dma = pltpu.SemaphoreType.DMA
        result = pl.pallas_call(
            functools.partial(kernel, planes, lines),
            out_shape=jax.ShapeDtypeStruct((slots, size, 1, width), jnp.float32),
            in_specs=[smem, hbm, hbm, hbm, hbm],
            out_specs=hbm,
            scratch_shapes=[
                square,
                pltpu.VMEM((6, slots, size, size), jnp.bfloat16),
                thin, thin, thin, thin, thin,
                square, square, square, square, square, square,
                wide, wide, wide, wide, wide,
                pltpu.VMEM((slots, size, 1, width), jnp.float32),
                dma((9,)),
                dma((slots,)),
                dma((3, slots)),
                dma((3, slots)),
                dma((2,)),
                dma((2,)),
                dma((slots,)),
                dma((slots,)),
                dma((slots,)),
                dma((slots,)),
                dma((slots,)),
            ],
            compiler_params=pltpu.CompilerParams(
                collective_id=0,
                has_side_effects=True,
                vmem_limit_bytes=60 * 1024 * 1024,
            ),
            cost_estimate=pl.CostEstimate(
                flops=18 * slots * size * size * width,
                bytes_accessed=16 * slots * size * size,
                transcendentals=0,
            ),
        )(slot_layer.reshape(slots), inverses, couplings,
          rhs.reshape(flat), previous.reshape(flat))
        result = pl.pallas_call(
            move,
            out_shape=jax.ShapeDtypeStruct(result.shape, result.dtype),
            in_specs=[hbm],
            out_specs=hbm,
            scratch_shapes=[
                pltpu.VMEM(result.shape, result.dtype), dma((slots,)), dma((slots,)),
            ],
            compiler_params=pltpu.CompilerParams(vmem_limit_bytes=60 * 1024 * 1024),
        )(result)
        return result.reshape(1, 1, *flat)

    return jax.shard_map(
        local,
        mesh=mesh,
        in_specs=(
            P("sweep", "span", None, None, None),
            P(None, "sweep", "span", None, None, None),
            P("sweep", "span", None, None, None),
            P("sweep", "span", None, None, None),
            P("sweep", "span", None),
        ),
        out_specs=P("sweep", "span", None, None, None),
        check_vma=False,
    )
```

profile of v0, /device:TPU:6, one launch (start us, length us, event | category | flops | bytes accessed | tf_op | source)
XLA Modules:
  0.0 27.4 jit_solution(14920362629414220185)
XLA Ops:
  0.0 25.6 %shard_map.55.src = f32[6,135,1,128]{3,2,1,0:T(1,128)} custom-call(s32[6]{0:T(128)} %bitcast.12, bf16[6,135,135]{2,1,0:T(8,128)(2,1)} %bitcast.9, bf16[6,6,135,135]{3,2,1,0:T(8,128)(2,1)} %bitcast.8, bf16[6,135,128]{2,1,0:T(8,128)(2,1)} %bitcast.10, bf16[6,135,128]{2,1,0:T(8,128)(2,1)} %bitcast.11), custom_call_target="tpu_custom_call" | custom-call | flops 251942400 | bytes 1749600 | tf_op jit(solution)/shard_map/pallas_call | solution.py:274
  25.6 1.8 %shard_map.56 = f32[6,135,1,128]{3,2,1,0:T(1,128)} custom-call(f32[6,135,1,128]{3,2,1,0:T(1,128)} %shard_map.55.src), custom_call_target="tpu_custom_call" | custom-call | tf_op jit(solution)/shard_map/pallas_call | solution.py:310
where the time goes:
time: 27.5 us; the launch traced here: 27.4 us
  Pallas kernels  27.3 us (99%)
    pallas_call x1, Pallas kernels, local(): pl.pallas_call(functools.partial(kernel, planes, lines), out_shape=jax.Sh...  25.6 us
    pallas_call x1, Pallas kernels, local(): pl.pallas_call(move, out_shape=jax.ShapeDtypeStruct(result.shape, result....  1.78 us

commit v1 on v0

--- a/solution.py
+++ b/solution.py
@@ -101,9 +101,12 @@
     def relay(s):
         return send(fresh.at[s], inflow.at[s], relay_send.at[s], relay_recv.at[s], ahead)
 
-    for s in range(slots):
-        halo(0, s).start()
-        halo(1, s).start()
+    def send_halo():
+        for s in range(slots):
+            halo(0, s).start()
+            halo(1, s).start()
+
+    pl.when(even)(send_halo)
 
     @pl.when(has_up)
     def _():
@@ -118,6 +121,8 @@
     faces[0].wait()
     for s in range(slots):
         high[s], low[s] = split(-mul(inv[s], coup[0, s]))
+
+    pl.when(odd)(send_halo)
 
     @pl.when(jnp.logical_and(even, later))
     def _():

time: 27.5 us -> 27.6 us (level); the launches traced: 27.4 us -> 27.1 us
  no operation moved by 1% of the time
where the time goes in v1:
time: 27.6 us; the launch traced here: 27.1 us
  Pallas kernels  27.1 us (98%)
    pallas_call x1, Pallas kernels, local(): pl.pallas_call(functools.partial(kernel, planes, lines), out_shape=jax.Sh...  25.3 us
    pallas_call x1, Pallas kernels, local(): pl.pallas_call(move, out_shape=jax.ShapeDtypeStruct(result.shape, result....  1.78 us

profile of v1, /device:TPU:6, one launch (start us, length us, event | category | flops | bytes accessed | tf_op | source)
XLA Modules:
  0.0 27.1 jit_solution(16748722631872974528)
XLA Ops:
  0.0 25.3 %shard_map.55.src = f32[6,135,1,128]{3,2,1,0:T(1,128)} custom-call(s32[6]{0:T(128)} %bitcast.12, bf16[6,135,135]{2,1,0:T(8,128)(2,1)} %bitcast.9, bf16[6,6,135,135]{3,2,1,0:T(8,128)(2,1)} %bitcast.8, bf16[6,135,128]{2,1,0:T(8,128)(2,1)} %bitcast.10, bf16[6,135,128]{2,1,0:T(8,128)(2,1)} %bitcast.11), custom_call_target="tpu_custom_call" | custom-call | flops 251942400 | bytes 1749600 | tf_op jit(solution)/shard_map/pallas_call | solution.py:279
  25.3 1.8 %shard_map.56 = f32[6,135,1,128]{3,2,1,0:T(1,128)} custom-call(f32[6,135,1,128]{3,2,1,0:T(1,128)} %shard_map.55.src), custom_call_target="tpu_custom_call" | custom-call | tf_op jit(solution)/shard_map/pallas_call | solution.py:315
